TPU v7x, 1024 devices: a whole 8x8x8 slice. The times are simulated.
1024 devices in a mesh: dp: 64 (over z, y_hi, core), seq: 16 (over y_lo, x).
Axes of the slice: x: 8, y: 8 (y_hi: 4, y_lo: 2; y = y_hi * 2 + y_lo), z: 8, core: 2. Of those that a mesh axis runs over, the one named last changes fastest.
Arguments:
- enc_final: bfloat16 [64, 384, 4096], P('dp', 'seq'), may hold values from -6 to 6
- norm_gain: float32 [4096], replicated, may hold values from 0.1 to 1.9
- dec_queries: bfloat16 [2, 64, 2048, 2048], P(None, 'dp', 'seq'), may hold values from -48 to 48
- out_grad: bfloat16 [2, 64, 2048, 2048], P(None, 'dp', 'seq'), may hold values from -6 to 6
- enc_keys: bfloat16 [2, 64, 384, 2048], P(None, 'dp', 'seq'), may hold values from -6 to 6
- enc_values: bfloat16 [2, 64, 384, 2048], P(None, 'dp', 'seq'), may hold values from -6 to 6
- key_weight: bfloat16 [2, 4096, 2048], P(None, None, 'seq'), may hold values from -0.09375 to 0.09375
- value_weight: bfloat16 [2, 4096, 2048], P(None, None, 'seq'), may hold values from -0.09375 to 0.09375
Outputs:
- enc_grad: bfloat16 [64, 384, 4096], P('dp', 'seq')
- gain_grad: float32 [4096], replicated
All inputs are finite; a program needn't handle non-finite values.
Results may differ from a plain program's by a relative error of at most 0.007.
Values may be sent and summed in bfloat16 or wider, within the bound.
A program may use at most 128 MiB of HBM per device.

v0:
```python
import jax
import jax.numpy as jnp
from jax import lax
from jax.sharding import PartitionSpec as P

HEAD_DIM = 64


def split_up(x, dim, length):
    lengths = x.shape
    tiles = x.reshape(*lengths[:dim], length, lengths[dim] // length, *lengths[dim + 1 :])
    return jnp.moveaxis(tiles, dim, 0)


def summed_on_arrival(x, axis, dim):
    length = lax.axis_size(axis)
    tiles = lax.all_to_all(split_up(x, dim, length), axis, 0, 0, tiled=True)
    return jnp.sum(tiles, axis=0)


def copy_for_each(x, axis):
    length = lax.axis_size(axis)
    return lax.all_to_all(jnp.broadcast_to(x[None], (length, *x.shape)), axis, 0, 0, tiled=True)


def of_everyone(x, axis):
    everything = copy_for_each(x, axis)
    return jnp.sum(everything, axis=0)


def head_grads(query_rows, grad_rows, key_rows, value_rows, head_size):
    dec_count = query_rows.shape[0]
    enc_count = key_rows.shape[0]
    head_count = query_rows.shape[1] // head_size
    query_heads = query_rows.reshape(dec_count, head_count, head_size)
    grad_heads = grad_rows.reshape(dec_count, head_count, head_size)
    key_heads = key_rows.reshape(enc_count, head_count, head_size)
    value_heads = value_rows.reshape(enc_count, head_count, head_size)
    scores = jnp.einsum("qhd,khd->hqk", query_heads, key_heads, preferred_element_type=jnp.float32)
    row_peak = jnp.max(scores, axis=-1, keepdims=True)
    shifted = jnp.exp(scores - row_peak)
    weights = shifted / jnp.sum(shifted, axis=-1, keepdims=True)
    prob_grad = jnp.einsum(
        "qhd,khd->hqk", grad_heads, value_heads, preferred_element_type=jnp.float32
    )
    row_delta = jnp.sum(weights * prob_grad, axis=-1, keepdims=True)
    score_grad = (weights * (prob_grad - row_delta)).astype(jnp.bfloat16)
    value_grad = jnp.einsum(
        "hqk,qhd->khd", weights.astype(jnp.bfloat16), grad_heads, preferred_element_type=jnp.float32
    )
    key_grad = jnp.einsum(
        "hqk,qhd->khd", score_grad, query_heads, preferred_element_type=jnp.float32
    )
    return (key_grad.reshape(enc_count, -1), value_grad.reshape(enc_count, -1))


def body(
    enc_final, norm_gain, dec_queries, out_grad, enc_keys, enc_values, key_weight, value_weight
):
    layer_count = dec_queries.shape[0]
    head_size = HEAD_DIM
    key_parts = []
    value_parts = []
    for layer_index in range(layer_count):
        query_rows = dec_queries[layer_index, 0]
        grad_rows = out_grad[layer_index, 0]
        key_rows = enc_keys[layer_index, 0]
        value_rows = enc_values[layer_index, 0]
        query_cols, grad_cols, key_cols, value_cols = (
            lax.all_to_all(query_rows, "seq", split_axis=1, concat_axis=0, tiled=True),
            lax.all_to_all(grad_rows, "seq", split_axis=1, concat_axis=0, tiled=True),
            lax.all_to_all(key_rows, "seq", split_axis=1, concat_axis=0, tiled=True),
            lax.all_to_all(value_rows, "seq", split_axis=1, concat_axis=0, tiled=True),
        )
        key_sum, value_sum = head_grads(query_cols, grad_cols, key_cols, value_cols, head_size)
        key_parts.append(key_sum.astype(jnp.bfloat16))
        value_parts.append(value_sum.astype(jnp.bfloat16))
    model_width = enc_final.shape[2]
    running = jnp.zeros((lax.axis_size("seq") * enc_final.shape[1], model_width), jnp.float32)
    for layer_index in range(layer_count):
        key_slice = key_parts[layer_index]
        value_slice = value_parts[layer_index]
        running = running + jnp.einsum(
            "rc,dc->rd", key_slice, key_weight[layer_index], preferred_element_type=jnp.float32
        )
        running = running + jnp.einsum(
            "rc,dc->rd", value_slice, value_weight[layer_index], preferred_element_type=jnp.float32
        )
    state_grad = lax.psum_scatter(running, "seq", scatter_dimension=0, tiled=True)
    final_float = enc_final[0].astype(jnp.float32)
    inv_rms = lax.rsqrt(jnp.mean(final_float * final_float, axis=-1, keepdims=True) + 1e-06)
    normed = final_float * inv_rms
    scaled = norm_gain[None, :] * state_grad
    grad_rows_out = inv_rms * (scaled - normed * jnp.mean(scaled * normed, axis=-1, keepdims=True))
    gain_term = jnp.sum(state_grad * normed, axis=0)
    gain_piece = summed_on_arrival(gain_term, "seq", 0)
    gain_piece = of_everyone(gain_piece, "dp")
    gain_total = lax.all_gather(gain_piece, "seq", axis=0, tiled=True)
    gain_grad = gain_total / lax.axis_size("dp")
    return (grad_rows_out.astype(jnp.bfloat16)[None], gain_grad)


def solution(mesh):
    placed = (
        P("dp", "seq", None),
        P(),
        P(None, "dp", "seq", None),
        P(None, "dp", "seq", None),
        P(None, "dp", "seq", None),
        P(None, "dp", "seq", None),
        P(None, None, "seq"),
        P(None, None, "seq"),
    )
    return jax.shard_map(
        body, mesh=mesh, in_specs=placed, out_specs=(P("dp", "seq", None), P()), check_vma=False
    )
```

profile of v0, /device:TPU:1, one launch (start us, length us, event | category | flops | bytes accessed | tf_op | source)
XLA Modules:
  0.0 354.3 jit_solution(12977012552576823834)
XLA Ops:
  7.2 1.0 slice_bitcast_fusion.3
  8.9 8.5 %all-to-all-start.1 = ((bf16[24,16,128]{2,0,1:T(8,128)(2,1)}), bf16[24,16,128]{2,0,1:T(8,128)(2,1)S(1)}, u32[]{:S(2)}, u32[]{:S(2)}) async-start(bf16[24,16,128]{2,0,1:T(8,128)(2,1)} %copy.80), calls=%async_computation.1 | async-start | bytes 196608 | tf_op jit(solution)/shard_map/all_to_all | solution.py:72
  18.1 6.7 %all-to-all-done.1 = bf16[24,16,128]{2,0,1:T(8,128)(2,1)S(1)} async-done(((bf16[24,16,128]{2,0,1:T(8,128)(2,1)}), bf16[24,16,128]{2,0,1:T(8,128)(2,1)S(1)}, u32[]{:S(2)}, u32[]{:S(2)}) %all-to-all-start.1) | async-done | bytes 98336 | tf_op jit(solution)/shard_map/all_to_all | solution.py:72
  24.9 3.5 all-to-all-start.5
  28.4 1.0 slice_bitcast_fusion.2
  30.0 5.8 %all-to-all-done.5 = bf16[24,16,128]{2,0,1:T(8,128)(2,1)S(1)} async-done(((bf16[24,16,128]{2,0,1:T(8,128)(2,1)}), bf16[24,16,128]{2,0,1:T(8,128)(2,1)S(1)}, u32[]{:S(2)}, u32[]{:S(2)}) %all-to-all-start.5) | async-done | bytes 98336 | tf_op jit(solution)/shard_map/all_to_all | solution.py:72
  35.8 3.5 all-to-all-start.3
  40.0 6.9 %all-to-all-done.3 = bf16[24,16,128]{2,0,1:T(8,128)(2,1)S(1)} async-done(((bf16[24,16,128]{2,0,1:T(8,128)(2,1)}), bf16[24,16,128]{2,0,1:T(8,128)(2,1)S(1)}, u32[]{:S(2)}, u32[]{:S(2)}) %all-to-all-start.3) | async-done | bytes 98336 | tf_op jit(solution)/shard_map/all_to_all | solution.py:73
  46.9 3.5 all-to-all-start.7
  50.4 1.3 fusion.94
  51.7 1.0 copy.78
  52.7 5.1 %all-to-all-done.7 = bf16[24,16,128]{2,0,1:T(8,128)(2,1)S(1)} async-done(((bf16[24,16,128]{2,0,1:T(8,128)(2,1)}), bf16[24,16,128]{2,0,1:T(8,128)(2,1)S(1)}, u32[]{:S(2)}, u32[]{:S(2)}) %all-to-all-start.7) | async-done | bytes 98336 | tf_op jit(solution)/shard_map/all_to_all | solution.py:73
  57.8 3.6 %all-to-all-start = ((bf16[128,16,128]{0,2,1:T(8,128)(2,1)}), bf16[128,16,128]{0,2,1:T(8,128)(2,1)S(1)}, u32[]{:S(2)}, u32[]{:S(2)}) async-start(bf16[128,16,128]{0,2,1:T(8,128)(2,1)} %bitcast.1), calls=%async_computation | async-start | bytes 1048576 | tf_op jit(solution)/shard_map/all_to_all | solution.py:70
  61.4 1.0 copy.88
  62.4 9.8 %all-to-all-done = bf16[128,16,128]{0,2,1:T(8,128)(2,1)S(1)} async-done(((bf16[128,16,128]{0,2,1:T(8,128)(2,1)}), bf16[128,16,128]{0,2,1:T(8,128)(2,1)S(1)}, u32[]{:S(2)}, u32[]{:S(2)}) %all-to-all-start) | async-done | bytes 524320 | tf_op jit(solution)/shard_map/all_to_all | solution.py:70
  72.2 4.8 %all-to-all-start.4 = ((bf16[128,16,128]{0,2,1:T(8,128)(2,1)}), bf16[128,16,128]{0,2,1:T(8,128)(2,1)S(1)}, u32[]{:S(2)}, u32[]{:S(2)}) async-start(bf16[128,16,128]{0,2,1:T(8,128)(2,1)} %bitcast.13), calls=%async_computation.4 | async-start | bytes 1048576 | tf_op jit(solution)/shard_map/all_to_all | solution.py:70
  77.1 1.0 copy.82
  78.1 14.8 %all-to-all-done.4 = bf16[128,16,128]{0,2,1:T(8,128)(2,1)S(1)} async-done(((bf16[128,16,128]{0,2,1:T(8,128)(2,1)}), bf16[128,16,128]{0,2,1:T(8,128)(2,1)S(1)}, u32[]{:S(2)}, u32[]{:S(2)}) %all-to-all-start.4) | async-done | bytes 524320 | tf_op jit(solution)/shard_map/all_to_all | solution.py:70
  92.9 4.6 %all-to-all-start.2 = ((bf16[128,16,128]{0,2,1:T(8,128)(2,1)}), bf16[128,16,128]{0,2,1:T(8,128)(2,1)S(1)}, u32[]{:S(2)}, u32[]{:S(2)}) async-start(bf16[128,16,128]{0,2,1:T(8,128)(2,1)} %bitcast.4), calls=%async_computation.2 | async-start | bytes 1048576 | tf_op jit(solution)/shard_map/all_to_all | solution.py:71
  97.5 1.0 copy.92
  98.5 12.3 %all-to-all-done.2 = bf16[128,16,128]{0,2,1:T(8,128)(2,1)S(1)} async-done(((bf16[128,16,128]{0,2,1:T(8,128)(2,1)}), bf16[128,16,128]{0,2,1:T(8,128)(2,1)S(1)}, u32[]{:S(2)}, u32[]{:S(2)}) %all-to-all-start.2) | async-done | bytes 524320 | tf_op jit(solution)/shard_map/all_to_all | solution.py:71
  110.8 7.0 %all-to-all-start.6 = ((bf16[128,16,128]{0,2,1:T(8,128)(2,1)}), bf16[128,16,128]{0,2,1:T(8,128)(2,1)S(1)}, u32[]{:S(2)}, u32[]{:S(2)}) async-start(bf16[128,16,128]{0,2,1:T(8,128)(2,1)} %bitcast.16), calls=%async_computation.6 | async-start | bytes 1048576 | tf_op jit(solution)/shard_map/all_to_all | solution.py:71
  118.2 1.0 reshape.112
  119.2 1.7 reshape.110
  120.9 1.0 reshape.114
  123.4 1.1 reshape.109
  124.5 7.0 %all-to-all-done.6 = bf16[128,16,128]{0,2,1:T(8,128)(2,1)S(1)} async-done(((bf16[128,16,128]{0,2,1:T(8,128)(2,1)}), bf16[128,16,128]{0,2,1:T(8,128)(2,1)S(1)}, u32[]{:S(2)}, u32[]{:S(2)}) %all-to-all-start.6) | async-done | bytes 524320 | tf_op jit(solution)/shard_map/all_to_all | solution.py:71
  132.0 4.5 %fusion.95 = (f32[2,2048]{1,0:T(2,128)S(1)}, f32[2,2048,384]{1,2,0:T(8,128)}) fusion(bf16[2048,2,64]{0,2,1:T(8,128)(2,1)S(1)} %reshape.111, bf16[384,2,64]{2,1,0:T(2,128)(2,1)S(1)} %reshape.112), kind=kOutput, calls=%fused_computation.69 | convolution fusion | flops 204472704 | bytes 6930432 | tf_op jit(solution)/shard_map/sub | solution.py:41
  136.5 3.0 fusion.13
  139.5 7.0 %multiply_reduce_fusion = (f32[2,2048]{1,0:T(2,128)}, f32[2,2048,384]{1,2,0:T(8,128)}) fusion(f32[2,2048,384]{1,2,0:T(8,128)} %get-tuple-element.13, f32[2,2048]{1,0:T(2,128)S(1)} %get-tuple-element.12, bf16[2048,2,64]{0,2,1:T(8,128)(2,1)S(1)} %reshape.113, bf16[384,2,64]{2,1,0:T(2,128)(2,1)S(1)} %reshape.114), kind=kOutput, calls=%fused_computation.4 | convolution fusion | flops 206041088 | bytes 13238272 | tf_op jit(solution)/shard_map/qhd,khd->hqk/dot_general | solution.py:43
  146.5 6.1 %fusion.16 = bf16[2,384,64]{1,2,0:T(8,128)(2,1)} fusion(bf16[2048,2,64]{0,2,1:T(8,128)(2,1)S(1)} %reshape.111, f32[2,2048,384]{1,2,0:T(8,128)} %get-tuple-element.15, f32[2,2048]{1,0:T(2,128)} %get-tuple-element.14, f32[2,2048]{1,0:T(2,128)S(1)} %get-tuple-element.12, bf16[384,2,64]{2,1,0:T(2,128)(2,1)S(1)} %reshape.112), kind=kOutput, calls=%fused_computation.21 | convolution fusion | flops 410571136 | bytes 7045120 | tf_op jit(solution)/shard_map/hqk,qhd->khd/dot_general | solution.py:51
  152.6 4.6 %fusion.19 = f32[384,4096]{1,0:T(8,128)} fusion(bf16[384,128]{0,1:T(8,128)(2,1)} %bitcast.106, bf16[2,4096,128]{2,1,0:T(8,128)(2,1)S(1)} %copy-done), kind=kOutput, calls=%fused_computation.24 | convolution fusion | flops 402653184 | bytes 7438336 | tf_op jit(solution)/shard_map/rc,dc->rd/dot_general | solution.py:83
  157.2 4.5 %fusion.98 = (f32[2,2048]{1,0:T(2,128)S(1)}, f32[2,2048,384]{1,2,0:T(8,128)}) fusion(bf16[2048,2,64]{0,2,1:T(8,128)(2,1)S(1)} %reshape.107, bf16[384,2,64]{2,1,0:T(2,128)(2,1)S(1)} %reshape.108), kind=kOutput, calls=%fused_computation.70 | convolution fusion | flops 204472704 | bytes 6930432 | tf_op jit(solution)/shard_map/sub | solution.py:41
  162.0 3.0 fusion.10
  165.0 7.0 %multiply_reduce_fusion.1 = (f32[2,2048]{1,0:T(2,128)}, f32[2,2048,384]{1,2,0:T(8,128)}) fusion(f32[2,2048,384]{1,2,0:T(8,128)} %get-tuple-element.17, f32[2,2048]{1,0:T(2,128)S(1)} %get-tuple-element.16, bf16[2048,2,64]{0,2,1:T(8,128)(2,1)S(1)} %copy-done.4, bf16[384,2,64]{2,1,0:T(2,128)(2,1)S(1)} %copy-done.8), kind=kOutput, calls=%fused_computation.7 | convolution fusion | flops 206041088 | bytes 13238272 | tf_op jit(solution)/shard_map/qhd,khd->hqk/dot_general | solution.py:43
  172.0 5.3 %fusion.17 = bf16[2,384,64]{1,2,0:T(8,128)(2,1)S(1)} fusion(bf16[2048,2,64]{0,2,1:T(8,128)(2,1)S(1)} %reshape.107, f32[2,2048,384]{1,2,0:T(8,128)} %get-tuple-element.19, f32[2,2048]{1,0:T(2,128)} %get-tuple-element.18, f32[2,2048]{1,0:T(2,128)S(1)} %get-tuple-element.16, bf16[384,2,64]{2,1,0:T(2,128)(2,1)S(1)} %reshape.108), kind=kOutput, calls=%fused_computation.22 | convolution fusion | flops 410571136 | bytes 7045120 | tf_op jit(solution)/shard_map/hqk,qhd->khd/dot_general | solution.py:51
  177.3 1.0 fusion.23
  178.8 1.0 fusion.21
  180.9 3.7 %add_add_fusion = f32[384,4096]{1,0:T(8,128)} fusion(f32[384,4096]{1,0:T(8,128)S(1)} %bitcast.92, f32[384,4096]{1,0:T(8,128)S(1)} %fusion.23, f32[384,4096]{1,0:T(8,128)S(1)} %fusion.21, bf16[384,128]{0,1:T(8,128)(2,1)S(1)} %bitcast.108, bf16[2,4096,128]{2,1,0:T(8,128)(2,1)S(1)} %copy-done.1), kind=kOutput, calls=%fused_computation.2 | convolution fusion | flops 407371776 | bytes 26312704 | tf_op jit(solution)/shard_map/rc,dc->rd/dot_general | solution.py:86
  184.7 0.9 copy-done.2
  185.8 88.9 %reduce-scatter.2.cloned.1.call-done = f32[24,4096]{1,0:T(8,128)} async-done(((f32[384,4096]{1,0:T(8,128)}), f32[24,4096]{1,0:T(8,128)}) %reduce-scatter.2.cloned.1.call-update) | async-done | bytes 393232 | tf_op jit(solution)/shard_map/reduce_scatter | solution.py:89
  274.7 1.8 fusion.40
  276.5 3.7 %all-to-all-start.8 = ((f32[16,1,256]{2,1,0:T(1,128)}), f32[16,1,256]{2,1,0:T(1,128)S(1)}, u32[]{:S(2)}, u32[]{:S(2)}) async-start(f32[16,1,256]{2,1,0:T(1,128)} %bitcast.27), calls=%async_computation.9 | async-start | bytes 32768 | tf_op jit(solution)/shard_map/all_to_all | solution.py:17
  280.2 7.3 %all-to-all-done.8 = f32[16,1,256]{2,1,0:T(1,128)S(1)} async-done(((f32[16,1,256]{2,1,0:T(1,128)}), f32[16,1,256]{2,1,0:T(1,128)S(1)}, u32[]{:S(2)}, u32[]{:S(2)}) %all-to-all-start.8) | async-done | bytes 16416 | tf_op jit(solution)/shard_map/all_to_all | solution.py:17
  288.2 23.1 %all-to-all-start.9 = ((f32[64,1,256]{2,1,0:T(1,128)}), f32[64,1,256]{2,1,0:T(1,128)S(1)}, u32[]{:S(2)}, u32[]{:S(2)}) async-start(f32[64,1,256]{2,1,0:T(1,128)} %broadcast_in_dim.5), calls=%async_computation.10 | async-start | bytes 131072 | tf_op jit(solution)/shard_map/all_to_all | solution.py:23
  311.3 1.8 fusion.42
  313.1 10.4 %all-to-all-done.9 = f32[64,1,256]{2,1,0:T(1,128)S(1)} async-done(((f32[64,1,256]{2,1,0:T(1,128)}), f32[64,1,256]{2,1,0:T(1,128)S(1)}, u32[]{:S(2)}, u32[]{:S(2)}) %all-to-all-start.9) | async-done | bytes 65568 | tf_op jit(solution)/shard_map/all_to_all | solution.py:23
  323.6 23.2 %all-gather = f32[16,1,256]{2,1,0:T(1,128)S(1)} all-gather(f32[1,1,256]{2,1,0:T(1,128)S(1)} %bitcast.110), channel_id=1, replica_groups=mesh['dp'=64,'seq'=16] {'seq'}, dimensions={0}, use_global_device_ids=true | all-gather | bytes 17408 | tf_op jit(solution)/shard_map/all_gather | solution.py:98
  (54 shorter events, 8.7 us)
Async XLA Ops:
  7.2 69.8 %copy-start.3 = (bf16[2,1,128,2048]{3,2,1,0:T(8,128)(2,1)S(1)}, bf16[2,1,128,2048]{3,2,1,0:T(8,128)(2,1)}, u32[]{:S(2)}) copy-start(bf16[2,1,128,2048]{3,2,1,0:T(8,128)(2,1)} %param.11) | copy-start | bytes 3145732
  8.9 16.0 %all-to-all-start.1 = ((bf16[24,16,128]{2,0,1:T(8,128)(2,1)}), bf16[24,16,128]{2,0,1:T(8,128)(2,1)S(1)}, u32[]{:S(2)}, u32[]{:S(2)}) async-start(bf16[24,16,128]{2,0,1:T(8,128)(2,1)} %copy.80), calls=%async_computation.1 | async-start | bytes 196608 | tf_op jit(solution)/shard_map/all_to_all | solution.py:72
  24.9 10.9 %all-to-all-start.5 = ((bf16[24,16,128]{2,0,1:T(8,128)(2,1)}), bf16[24,16,128]{2,0,1:T(8,128)(2,1)S(1)}, u32[]{:S(2)}, u32[]{:S(2)}) async-start(bf16[24,16,128]{2,0,1:T(8,128)(2,1)} %copy.90), calls=%async_computation.5 | async-start | bytes 196608 | tf_op jit(solution)/shard_map/all_to_all | solution.py:72
  35.8 82.4 %copy-start.5 = (bf16[24,16,128]{2,0,1:T(8,128)(2,1)}, bf16[24,16,128]{2,0,1:T(8,128)(2,1)S(1)}, u32[]{:S(2)}) copy-start(bf16[24,16,128]{2,0,1:T(8,128)(2,1)S(1)} %all-to-all-done.5) | copy-start | bytes 294916
  35.8 11.1 %all-to-all-start.3 = ((bf16[24,16,128]{2,0,1:T(8,128)(2,1)}), bf16[24,16,128]{2,0,1:T(8,128)(2,1)S(1)}, u32[]{:S(2)}, u32[]{:S(2)}) async-start(bf16[24,16,128]{2,0,1:T(8,128)(2,1)} %copy.84), calls=%async_computation.3 | async-start | bytes 196608 | tf_op jit(solution)/shard_map/all_to_all | solution.py:73
  46.9 63.9 %copy-start.6 = (bf16[24,16,128]{2,0,1:T(8,128)(2,1)}, bf16[24,16,128]{2,0,1:T(8,128)(2,1)S(1)}, u32[]{:S(2)}) copy-start(bf16[24,16,128]{2,0,1:T(8,128)(2,1)S(1)} %all-to-all-done.3) | copy-start | bytes 294916
  46.9 10.9 %all-to-all-start.7 = ((bf16[24,16,128]{2,0,1:T(8,128)(2,1)}), bf16[24,16,128]{2,0,1:T(8,128)(2,1)S(1)}, u32[]{:S(2)}, u32[]{:S(2)}) async-start(bf16[24,16,128]{2,0,1:T(8,128)(2,1)} %copy.94), calls=%async_computation.7 | async-start | bytes 196608 | tf_op jit(solution)/shard_map/all_to_all | solution.py:73
  57.8 60.3 %copy-start.7 = (bf16[24,16,128]{2,0,1:T(8,128)(2,1)}, bf16[24,16,128]{2,0,1:T(8,128)(2,1)S(1)}, u32[]{:S(2)}) copy-start(bf16[24,16,128]{2,0,1:T(8,128)(2,1)S(1)} %all-to-all-done.7) | copy-start | bytes 294916
  57.8 14.4 %all-to-all-start = ((bf16[128,16,128]{0,2,1:T(8,128)(2,1)}), bf16[128,16,128]{0,2,1:T(8,128)(2,1)S(1)}, u32[]{:S(2)}, u32[]{:S(2)}) async-start(bf16[128,16,128]{0,2,1:T(8,128)(2,1)} %bitcast.1), calls=%async_computation | async-start | bytes 1048576 | tf_op jit(solution)/shard_map/all_to_all | solution.py:70
  72.2 20.8 %all-to-all-start.4 = ((bf16[128,16,128]{0,2,1:T(8,128)(2,1)}), bf16[128,16,128]{0,2,1:T(8,128)(2,1)S(1)}, u32[]{:S(2)}, u32[]{:S(2)}) async-start(bf16[128,16,128]{0,2,1:T(8,128)(2,1)} %bitcast.13), calls=%async_computation.4 | async-start | bytes 1048576 | tf_op jit(solution)/shard_map/all_to_all | solution.py:70
  92.9 17.8 %all-to-all-start.2 = ((bf16[128,16,128]{0,2,1:T(8,128)(2,1)}), bf16[128,16,128]{0,2,1:T(8,128)(2,1)S(1)}, u32[]{:S(2)}, u32[]{:S(2)}) async-start(bf16[128,16,128]{0,2,1:T(8,128)(2,1)} %bitcast.4), calls=%async_computation.2 | async-start | bytes 1048576 | tf_op jit(solution)/shard_map/all_to_all | solution.py:71
  110.8 20.7 %all-to-all-start.6 = ((bf16[128,16,128]{0,2,1:T(8,128)(2,1)}), bf16[128,16,128]{0,2,1:T(8,128)(2,1)S(1)}, u32[]{:S(2)}, u32[]{:S(2)}) async-start(bf16[128,16,128]{0,2,1:T(8,128)(2,1)} %bitcast.16), calls=%async_computation.6 | async-start | bytes 1048576 | tf_op jit(solution)/shard_map/all_to_all | solution.py:71
  117.8 156.9 %reduce-scatter.2.cloned.1.call-start = ((), (), s32[]{:S(2)}) async-start(), calls=%async_computation.11 | async-start | bytes 6684672 | tf_op jit(solution)/shard_map/reduce_scatter | solution.py:89
  146.5 6.1 %copy-start = (bf16[2,4096,128]{2,1,0:T(8,128)(2,1)S(1)}, bf16[2,4096,128]{2,1,0:T(8,128)(2,1)}, u32[]{:S(2)}) copy-start(bf16[2,4096,128]{2,1,0:T(8,128)(2,1)} %param.14) | copy-start | bytes 6291460
  152.6 9.1 %copy-start.4 = (bf16[2048,2,64]{0,2,1:T(8,128)(2,1)S(1)}, bf16[2048,2,64]{0,2,1:T(8,128)(2,1)}, u32[]{:S(2)}) copy-start(bf16[2048,2,64]{0,2,1:T(8,128)(2,1)} %reshape.109) | copy-start | bytes 1572868
  161.7 3.2 copy-start.8
  177.2 1.6 copy-start.1
  177.2 1.6 copy-start.9
  177.2 2.8 slice-start
  178.3 1.9 copy-start.10
  178.8 2.1 slice-start.1
  184.7 0.9 copy-start.2
  184.7 90.0 %copy-start.11 = (f32[4096]{0:T(1024)S(1)}, f32[4096]{0:T(1024)}, u32[]{:S(2)}) copy-start(f32[4096]{0:T(1024)} %param.9) | copy-start | bytes 49156
  276.5 11.0 %all-to-all-start.8 = ((f32[16,1,256]{2,1,0:T(1,128)}), f32[16,1,256]{2,1,0:T(1,128)S(1)}, u32[]{:S(2)}, u32[]{:S(2)}) async-start(f32[16,1,256]{2,1,0:T(1,128)} %bitcast.27), calls=%async_computation.9 | async-start | bytes 32768 | tf_op jit(solution)/shard_map/all_to_all | solution.py:17
  288.2 35.3 %all-to-all-start.9 = ((f32[64,1,256]{2,1,0:T(1,128)}), f32[64,1,256]{2,1,0:T(1,128)S(1)}, u32[]{:S(2)}, u32[]{:S(2)}) async-start(f32[64,1,256]{2,1,0:T(1,128)} %broadcast_in_dim.5), calls=%async_computation.10 | async-start | bytes 131072 | tf_op jit(solution)/shard_map/all_to_all | solution.py:23
Sparse Core Ops, SparseCore 0:
  184.8 89.8 reduce-scatter.1
where the time goes:
time: 361 us; the launch traced here: 354 us
  waiting for transfers between devices  175 us (48%)
  starting transfers between devices  66.1 us (18%)
  matrix products  50.7 us (14%)
  blocking collectives  23.2 us (6%)
  local copies, waits for them, and re-layouts  20.5 us (6%)
  between operations  14.3 us (4%)
  other arithmetic  4.51 us (1%)
    reduce_scatter x1, waiting for transfers between devices, body(): lax.psum_scatter(running, 'seq', scatter_dimension=0, tiled=True)  88.9 us
    all_to_all x2, waiting for transfers between devices, body(): lax.all_to_all(query_rows, 'seq', split_axis=1, concat_axis=0, tiled=True)  24.6 us
    all_gather x1, blocking collectives, body(): gain_total = lax.all_gather(gain_piece, 'seq', axis=0, tiled=True)  23.2 us
    all_to_all x1, starting transfers between devices, copy_for_each(): lax.all_to_all(jnp.broadcast_to(x[None], (length, *x.shape)), axis, 0, 0,...  23.1 us
    all_to_all x2, waiting for transfers between devices, body(): lax.all_to_all(grad_rows, 'seq', split_axis=1, concat_axis=0, tiled=True)  19.2 us
    dot_general x2, matrix products, head_grads(): jnp.einsum('qhd,khd->hqk', grad_heads, value_heads, preferred_element_typ...  14 us
    all_to_all x2, waiting for transfers between devices, body(): lax.all_to_all(key_rows, 'seq', split_axis=1, concat_axis=0, tiled=True)  12.5 us
    all_to_all x2, starting transfers between devices, body(): lax.all_to_all(key_rows, 'seq', split_axis=1, concat_axis=0, tiled=True)  12 us
  transfers between devices with their start and end apart: 11, of which 11 were waited for; matrix products, arithmetic and copies ran while one was open for 5% of the time, Pallas kernels for 0%

commit v1 on v0

v1 whole, which is shorter than its diff:
```python
import functools

import jax
import jax.numpy as jnp
from jax import lax
from jax.experimental import pallas as pl
from jax.experimental.pallas import tpu as pltpu
from jax.sharding import PartitionSpec as P

MESH = pl.DeviceIdType.MESH
HEAD_DIM = 64
LANES = 128
RING = 8
ROWS = 2
SHIFTS = (0, 4, 3, 5, 2, 6, 1, 7)
CHAINS = ((1, 0, 4, 0), (-1, 1, 4, 4), (1, 1, 3, 8), (-1, 0, 3, 11))
CHAIN_SLOTS = 14

TRANSPOSED = (((1,), (1,)), ((), ()))


def kernel(
    low_count, z_count,
    enc_ref, gain_ref, q_ref, g_ref, k_ref, v_ref, kw_ref, vw_ref,
    out_ref, gout_ref,
    qb, gb, kb, vb, km, vm, acc_k, acc_v, w, g_own, g_far, part, normed, inv,
    c_send, c_recv, a_send, a_recv, b_send, b_recv, z_send, z_recv, t_recv,
    tok_s, tok_r, kv_s, kv_r, own_s, w_s, w_r, f_s, f_r, x_s, x_r, c_s, c_r,
    a_s, a_r, b_s, b_r, z_s, z_r, t_s, t_r,
):
    layers = q_ref.shape[0]
    dec = q_ref.shape[2]
    enc = k_ref.shape[2]
    enc_all = enc * RING * ROWS
    width = enc_ref.shape[1]
    half = width // 2
    piece = width // (RING * ROWS)
    yh_count = low_count // 2

    seq = lax.axis_index("seq")
    dp = lax.axis_index("dp")
    x = lax.rem(seq, RING)
    y = seq // RING
    low = lax.rem(dp, low_count)
    z = dp // low_count
    core = lax.rem(low, 2)
    y_hi = low // 2

    def member(dx, dy):
        return lax.rem(y + dy, ROWS) * RING + lax.rem(x + dx + RING, RING)

    def columns(index, size):
        return pl.ds(pl.multiple_of(index * size, size), size)

    others = [(dx, dy) for dx in SHIFTS for dy in range(ROWS) if (dx, dy) != (0, 0)]
    across = member(0, 1)
    far_yh = lax.rem(y_hi + 2 * y - 1 + yh_count, yh_count)
    far_dp = z * low_count + far_yh * 2 + core
    low_dps = [z * low_count + lax.rem(low + j, low_count) for j in range(1, low_count)]
    z_dps = [lax.rem(z + j, z_count) * low_count + low for j in range(1, z_count)]

    barrier = pltpu.get_barrier_semaphore()
    for dx, dy in others:
        pl.semaphore_signal(
            barrier, inc=1, device_id={"seq": member(dx, dy)}, device_id_type=MESH
        )
    for other in low_dps + z_dps:
        pl.semaphore_signal(barrier, inc=1, device_id={"dp": other}, device_id_type=MESH)
    pl.semaphore_signal(
        barrier, inc=1, device_id={"dp": far_dp, "seq": across}, device_id_type=MESH
    )

    own = []
    for layer in range(layers):
        for n, (src, dst) in enumerate(((q_ref, qb), (g_ref, gb))):
            own.append(
                pltpu.make_async_copy(
                    src.at[layer, 0, :, columns(seq, LANES)],
                    dst.at[layer, 0, pl.ds(0, dec)],
                    tok_r.at[layer, n, 0, 0],
                )
            )
    own_kv = []
    for n, (src, dst) in enumerate(((k_ref, kb), (v_ref, vb))):
        own_kv.append(
            pltpu.make_async_copy(
                src.at[:, 0, :, columns(seq, LANES)], dst.at[seq], kv_r.at[n, 0, 0]
            )
        )
    own_w = []
    for layer in range(layers):
        for n, src in enumerate((kw_ref, vw_ref)):
            own_w.append(
                pltpu.make_async_copy(
                    src.at[layer],
                    w.at[:, pl.ds((2 * layer + n) * LANES, LANES)],
                    own_s.at[layer, n],
                )
            )
    for copy in own_kv + own + own_w:
        copy.start()

    pl.semaphore_wait(barrier, len(others) + len(low_dps) + len(z_dps) + 1)

    kv_copies = []
    for dx, dy in others:
        to = member(dx, dy)
        for n, (src, dst) in enumerate(((k_ref, kb), (v_ref, vb))):
            kv_copies.append(
                pltpu.make_async_remote_copy(
                    src.at[:, 0, :, columns(to, LANES)],
                    dst.at[seq],
                    kv_s.at[n, dx, dy],
                    kv_r.at[n, dx, dy],
                    device_id={"seq": to},
                    device_id_type=MESH,
                )
            )
    for copy in kv_copies:
        copy.start()

    w_dp = jnp.where(core == 0, dp, far_dp)
    w_copies = []
    for n, src in enumerate((kw_ref, vw_ref)):
        w_copies.append(
            pltpu.make_async_remote_copy(
                src.at[core],
                w.at[:, columns(2 * layers + 2 * core + n, LANES)],
                w_s.at[n],
                w_r.at[n],
                device_id={"dp": w_dp, "seq": across},
                device_id_type=MESH,
            )
        )

    tok_copies = []
    for layer in range(layers):
        for slot, dx in enumerate(SHIFTS):
            for dy in range(ROWS):
                if (dx, dy) == (0, 0):
                    continue
                to = member(dx, dy)
                for n, (src, dst) in enumerate(((q_ref, qb), (g_ref, gb))):
                    copy = pltpu.make_async_remote_copy(
                        src.at[layer, 0, :, columns(to, LANES)],
                        dst.at[layer, slot, pl.ds(dy * dec, dec)],
                        tok_s.at[layer, n, slot, dy],
                        tok_r.at[layer, n, slot, dy],
                        device_id={"seq": to},
                        device_id_type=MESH,
                    )
                    copy.start()
                    tok_copies.append(copy)
            if layer == 0 and slot == 1:
                for copy in w_copies:
                    copy.start()

    final = enc_ref[...].astype(jnp.float32)
    inv[...] = lax.rsqrt(jnp.mean(final * final, axis=-1, keepdims=True) + 1e-6)
    normed[...] = final * inv[...]

    for copy in own_kv:
        copy.wait()
    for copy in kv_copies:
        copy.wait_recv()

    first_head = lax.broadcasted_iota(jnp.int32, (enc_all, LANES), 1) < HEAD_DIM
    exchanges = []
    for layer in range(layers):
        for src, dst in ((kb, km), (vb, vm)):
            rows = src[:, layer].astype(jnp.float32).reshape(enc_all, LANES)
            dst[pl.ds(0, enc_all), :] = jnp.where(first_head, rows, 0.0).astype(jnp.bfloat16)
            dst[pl.ds(enc_all, enc_all), :] = jnp.where(first_head, 0.0, rows).astype(jnp.bfloat16)
        acc_k[...] = jnp.zeros_like(acc_k)
        acc_v[...] = jnp.zeros_like(acc_v)

        def tokens(slot, carry, layer=layer):
            for n, dst in enumerate((qb, gb)):
                for dy in range(ROWS):
                    there = dst.at[layer, slot, pl.ds(dy * dec, dec)]
                    pltpu.make_async_copy(there, there, tok_r.at[layer, n, slot, dy]).wait()
            queries = qb[layer, slot]
            grads = gb[layer, slot]
            count = queries.shape[0]
            scores = lax.dot_general(
                km[...], queries, TRANSPOSED, preferred_element_type=jnp.float32
            ).reshape(2, enc_all, count)
            prob_grad = lax.dot_general(
                vm[...], grads, TRANSPOSED, preferred_element_type=jnp.float32
            ).reshape(2, enc_all, count)
            shifted = jnp.exp(scores - jnp.max(scores, axis=1, keepdims=True))
            probs = shifted * (1.0 / jnp.sum(shifted, axis=1, keepdims=True))
            delta = jnp.sum(probs * prob_grad, axis=1, keepdims=True)
            score_grad = (probs * (prob_grad - delta)).astype(jnp.bfloat16)
            acc_v[...] += jnp.dot(
                probs.astype(jnp.bfloat16).reshape(2 * enc_all, count),
                grads,
                preferred_element_type=jnp.float32,
            )
            acc_k[...] += jnp.dot(
                score_grad.reshape(2 * enc_all, count),
                queries,
                preferred_element_type=jnp.float32,
            )
            return carry

        lax.fori_loop(0, RING, tokens, 0)

        side = enc_all // ROWS
        for n, acc in enumerate((acc_k, acc_v)):
            grad = jnp.where(
                first_head, acc[pl.ds(0, enc_all), :], acc[pl.ds(enc_all, enc_all), :]
            ).astype(jnp.bfloat16)
            for row in range(ROWS):
                g_own[row, :, pl.ds((2 * layer + n) * LANES, LANES)] = grad[
                    row * side : (row + 1) * side
                ]
        block = pl.ds(2 * layer * LANES, 2 * LANES)
        exchange = pltpu.make_async_remote_copy(
            g_own.at[1 - y, :, block],
            g_far.at[:, block],
            x_s.at[layer],
            x_r.at[layer],
            device_id={"seq": across},
            device_id_type=MESH,
        )
        exchange.start()
        exchanges.append(exchange)

        if layer == 0:
            for copy in own_w:
                copy.wait()
            for copy in w_copies:
                copy.wait()
            there = w.at[:, columns(layers + core, 2 * LANES)]
            handed = pltpu.make_async_remote_copy(
                there,
                there,
                f_s,
                f_r,
                device_id={"dp": dp + 1 - 2 * core},
                device_id_type=MESH,
            )
            handed.start()

    own_depth = 2 * layers * LANES
    tile = min(512, half)

    def project(first, grads, depth_start, add):
        def one(index, carry):
            at = first + index
            weights = w[columns(at, tile), pl.ds(depth_start, own_depth)]
            terms = lax.dot_general(
                grads, weights, TRANSPOSED, preferred_element_type=jnp.float32
            ).reshape(RING, enc, tile)
            if add:
                terms = terms + part[:, :, columns(at, tile)]
            part[:, :, columns(at, tile)] = terms
            return carry

        lax.fori_loop(0, half // tile, one, 0)

    mine = g_own[y]
    project(0, mine, 0, False)
    project(half // tile, mine, 0, False)
    handed.wait()
    for exchange in exchanges:
        exchange.wait_recv()
    theirs = g_far[...]

    hops = {}

    def term(dx, side_of):
        return part[lax.rem(x + dx + RING, RING), :, pl.ds(side_of * half, half)]

    def hop(chain, k):
        way, side_of, length, first = CHAINS[chain]
        total = term(way * (length - k), side_of)
        if k:
            hops[chain, k - 1].wait_recv()
            total = total + c_recv[first + k - 1].astype(jnp.float32)
        c_send[first + k] = total.astype(jnp.bfloat16)
        copy = pltpu.make_async_remote_copy(
            c_send.at[first + k],
            c_recv.at[first + k],
            c_s.at[first + k],
            c_r.at[first + k],
            device_id={"seq": member(way, 0)},
            device_id_type=MESH,
        )
        copy.start()
        hops[chain, k] = copy

    project(0, theirs, own_depth, True)
    hop(0, 0)
    hop(3, 0)
    project(half // tile, theirs, own_depth, True)
    hop(1, 0)
    hop(2, 0)
    for copy in kv_copies + tok_copies + exchanges:
        copy.wait_send()
    for k in range(1, 4):
        hop(0, k)
        hop(1, k)
        if k < 3:
            hop(2, k)
            hop(3, k)

    arrived = []
    for side_of in range(2):
        total = term(0, side_of)
        for chain, (way, chain_side, length, first) in enumerate(CHAINS):
            if chain_side == side_of:
                hops[chain, length - 1].wait_recv()
                total = total + c_recv[first + length - 1].astype(jnp.float32)
        arrived.append(total)

    a_copies = []
    for side_of in range(2):
        state = arrived[side_of]
        cols = pl.ds(side_of * half, half)
        part[0, :, cols] = state
        gains = jnp.sum(state * normed[:, cols], axis=0, keepdims=True)
        for s in range(RING):
            a_send[side_of * RING + s] = gains[:, s * piece : (s + 1) * piece]
    for j, (dx, dy) in enumerate(others):
        to = member(dx, dy)
        copy = pltpu.make_async_remote_copy(
            a_send.at[to],
            a_recv.at[j],
            a_s.at[j],
            a_r.at[j],
            device_id={"seq": to},
            device_id_type=MESH,
        )
        copy.start()
        a_copies.append(copy)

    state = part[0]
    scaled = gain_ref[...] * state
    mean = jnp.mean(scaled * normed[...], axis=-1, keepdims=True)
    out_ref[...] = (inv[...] * (scaled - normed[...] * mean)).astype(jnp.bfloat16)

    total = a_send[seq]
    for copy in a_copies:
        copy.wait_recv()
    for j in range(len(others)):
        total = total + a_recv[j]

    def everyone(total, send, recv, here, dps, ss, rs):
        send[...] = total
        recv[here] = total
        copies = []
        for j, other in enumerate(dps):
            copy = pltpu.make_async_remote_copy(
                send,
                recv.at[here],
                ss.at[j],
                rs.at[j],
                device_id={"dp": other},
                device_id_type=MESH,
            )
            copy.start()
            copies.append(copy)
        for copy in copies:
            copy.wait_recv()
        total = recv[0]
        for j in range(1, len(dps) + 1):
            total = total + recv[j]
        return total, copies

    total, b_copies = everyone(total, b_send, b_recv, low, low_dps, b_s, b_r)
    total, z_copies = everyone(total, z_send, z_recv, z, z_dps, z_s, z_r)

    t_recv[seq] = total * (1.0 / (low_count * z_count))
    t_copies = []
    for j, (dx, dy) in enumerate(others):
        copy = pltpu.make_async_remote_copy(
            t_recv.at[seq],
            t_recv.at[seq],
            t_s.at[j],
            t_r.at[j],
            device_id={"seq": member(dx, dy)},
            device_id_type=MESH,
        )
        copy.start()
        t_copies.append(copy)
    for copy in list(hops.values()) + a_copies + b_copies + z_copies:
        copy.wait_send()
    for copy in t_copies:
        copy.wait()
    for s in range(RING * ROWS):
        gout_ref[:, pl.ds(s * piece, piece)] = t_recv[s]


def body(low_count, z_count, enc_final, norm_gain, q, g, k, v, kw, vw):
    enc, width = enc_final.shape[1:]
    layers, _, dec, _ = q.shape
    group = RING * ROWS
    enc_all = enc * group
    half = width // 2
    piece = width // group
    bf, f32 = jnp.bfloat16, jnp.float32
    dma = pltpu.SemaphoreType.DMA
    vmem = pltpu.VMEM
    outs = pl.pallas_call(
        functools.partial(kernel, low_count, z_count),
        out_shape=(
            jax.ShapeDtypeStruct((enc, width), bf),
            jax.ShapeDtypeStruct((1, width), f32),
        ),
        in_specs=[pl.BlockSpec(memory_space=vmem)] * 2 + [pl.BlockSpec(memory_space=pl.ANY)] * 6,
        out_specs=(pl.BlockSpec(memory_space=vmem),) * 2,
        scratch_shapes=[
            vmem((layers, RING, ROWS * dec, LANES), bf),
            vmem((layers, RING, ROWS * dec, LANES), bf),
            vmem((group, layers, enc, LANES), bf),
            vmem((group, layers, enc, LANES), bf),
            vmem((2 * enc_all, LANES), bf),
            vmem((2 * enc_all, LANES), bf),
            vmem((2 * enc_all, LANES), f32),
            vmem((2 * enc_all, LANES), f32),
            vmem((width, 4 * layers * LANES), bf),
            vmem((ROWS, enc_all // ROWS, 2 * layers * LANES), bf),
            vmem((enc_all // ROWS, 2 * layers * LANES), bf),
            vmem((RING, enc, width), f32),
            vmem((enc, width), f32),
            vmem((enc, 1), f32),
            vmem((CHAIN_SLOTS, enc, half), bf),
            vmem((CHAIN_SLOTS, enc, half), bf),
            vmem((group, 1, piece), f32),
            vmem((group, 1, piece), f32),
            vmem((1, piece), f32),
            vmem((low_count, 1, piece), f32),
            vmem((1, piece), f32),
            vmem((z_count, 1, piece), f32),
            vmem((group, 1, piece), f32),
            dma((layers, 2, RING, ROWS)),
            dma((layers, 2, RING, ROWS)),
            dma((2, RING, ROWS)),
            dma((2, RING, ROWS)),
            dma((layers, 2)),
            dma((2,)),
            dma((2,)),
            dma(()),
            dma(()),
            dma((layers,)),
            dma((layers,)),
            dma((CHAIN_SLOTS,)),
            dma((CHAIN_SLOTS,)),
            dma((group,)),
            dma((group,)),
            dma((low_count,)),
            dma((low_count,)),
            dma((z_count,)),
            dma((z_count,)),
            dma((group,)),
            dma((group,)),
        ],
        compiler_params=pltpu.CompilerParams(
            collective_id=0, has_side_effects=True, vmem_limit_bytes=56 * 2**20
        ),
    )(enc_final[0], norm_gain[None], q, g, k, v, kw, vw)
    return outs[0][None], outs[1][0]


def solution(mesh):
    count = mesh.shape["dp"]
    low_count = min(8, count)
    placed = (
        P("dp", "seq", None),
        P(),
        P(None, "dp", "seq", None),
        P(None, "dp", "seq", None),
        P(None, "dp", "seq", None),
        P(None, "dp", "seq", None),
        P(None, None, "seq"),
        P(None, None, "seq"),
    )
    return jax.shard_map(
        functools.partial(body, low_count, count // low_count),
        mesh=mesh,
        in_specs=placed,
        out_specs=(P("dp", "seq", None), P()),
        check_vma=False,
    )
```

time: 361 us -> 131 us (0.36); the launches traced: 354 us -> 131 us
  waiting for transfers between devices: 175 us -> 0 us
  Pallas kernels: 0 us -> 127 us
  starting transfers between devices: 66.1 us -> 0 us
  matrix products: 50.7 us -> 0 us
  blocking collectives: 23.2 us -> 0 us
  local copies, waits for them, and re-layouts: 20.5 us -> 2.94 us
  between operations: 14.3 us -> 0.64 us
  other arithmetic: 4.51 us -> 0 us
    pallas_call x0 -> x1, Pallas kernels: none -> 127 us  [body(): pl.pallas_call(functools.partial(kernel, low_count, z_count), out_shape=(...]
    reduce_scatter x1 -> x0, waiting for transfers between devices: 88.9 us -> none  [body(): lax.psum_scatter(running, 'seq', scatter_dimension=0, tiled=True)]
    all_to_all x10 -> x0, waiting for transfers between devices: 86 us -> none  [the longest x2 24.6 us: body(): lax.all_to_all(query_rows, 'seq', split_axis=1, concat_axis=0, tiled=True)]
    all_to_all x10 -> x0, starting transfers between devices: 65.8 us -> none  [the longest x1 23.1 us: copy_for_each(): lax.all_to_all(jnp.broadcast_to(x[None], (length, *x.shape)), axis, 0, 0,...]
    dot_general x10 -> x0, matrix products: 41.7 us -> none  [the longest x2 14 us: head_grads(): jnp.einsum('qhd,khd->hqk', grad_heads, value_heads, preferred_element_typ...]
    all_gather x1 -> x0, blocking collectives: 23.2 us -> none  [body(): gain_total = lax.all_gather(gain_piece, 'seq', axis=0, tiled=True)]
    sub x2 -> x0, matrix products: 8.99 us -> none  [head_grads(): shifted = jnp.exp(scores - row_peak)]
    reshape x8 -> x0, local copies, waits for them, and re-layouts: 5.55 us -> none  [the longest x2 2.7 us: head_grads(): value_heads = value_rows.reshape(enc_count, head_count, head_size)]
  transfers between devices with their start and end apart: 11 -> 0, of which waited for: 11 -> 0; matrix products, arithmetic and copies ran while one was open for 5% -> 0% of each run, Pallas kernels for 0% -> 0%
where the time goes in v1:
time: 131 us
  Pallas kernels  127 us (97%)
  local copies, waits for them, and re-layouts  2.94 us (2%)
    pallas_call x1, Pallas kernels, body(): pl.pallas_call(functools.partial(kernel, low_count, z_count), out_shape=(...  127 us
    unnamed x2, local copies, waits for them, and re-layouts  2.94 us

profile of v1, /device:TPU:1, one launch (start us, length us, event | category | flops | bytes accessed | tf_op | source)
XLA Modules:
  0.0 130.9 jit_solution(11522146291790373481)
XLA Ops:
  0.6 127.3 %shard_map.95 = (bf16[24,4096]{1,0:T(8,128)(2,1)}, f32[1,4096]{1,0:T(1,128)}) custom-call(bf16[24,4096]{1,0:T(8,128)(2,1)} %bitcast.5, f32[1,4096]{1,0:T(1,128)} %bitcast.6, bf16[2,1,128,2048]{3,2,1,0:T(8,128)(2,1)} %q_ref.1, bf16[2,1,128,2048]{3,2,1,0:T(8,128)(2,1)} %g_ref.1, bf16[2,1,24,2048]{3,2,1,0:T(8,128)(2,1)} %k_ref.1, ...), custom_call_target="tpu_custom_call" | custom-call | tf_op jit(solution)/shard_map/pallas_call | solution.py:406
  127.9 1.6 %copy.12 = bf16[1,24,4096]{2,1,0:T(8,128)(2,1)} copy(bf16[1,24,4096]{2,1,0:T(8,128)(2,1)} %bitcast.4) | data formatting | bytes 393216
  129.5 1.3 %copy.13 = f32[4096]{0:T(1024)} copy(f32[4096]{0:T(1024)} %bitcast.7) | data formatting | bytes 32768

commit v2 on v1

--- a/solution.py
+++ b/solution.py
@@ -13,8 +13,10 @@
 RING = 8
 ROWS = 2
 SHIFTS = (0, 4, 3, 5, 2, 6, 1, 7)
-CHAINS = ((1, 0, 4, 0), (-1, 1, 4, 4), (1, 1, 3, 8), (-1, 0, 3, 11))
-CHAIN_SLOTS = 14
+PARTS = (0, 2, 1, 3)
+HOPS = ((4, 3), (4, 3), (3, 4), (3, 4))
+FIRST = tuple(tuple(sum(h[0] + h[1] for h in HOPS[:p]) + d * HOPS[p][0] for d in (0, 1)) for p in range(4))
+CHAIN_SLOTS = sum(h[0] + h[1] for h in HOPS)
 
 TRANSPOSED = (((1,), (1,)), ((), ()))
 
@@ -23,7 +25,7 @@
     low_count, z_count,
     enc_ref, gain_ref, q_ref, g_ref, k_ref, v_ref, kw_ref, vw_ref,
     out_ref, gout_ref,
-    qb, gb, kb, vb, km, vm, acc_k, acc_v, w, g_own, g_far, part, normed, inv,
+    qb, gb, kb, vb, km, vm, acc_k, acc_v, w, g_own, g_far, part, final_state, normed, inv,
     c_send, c_recv, a_send, a_recv, b_send, b_recv, z_send, z_recv, t_recv,
     tok_s, tok_r, kv_s, kv_r, own_s, w_s, w_r, f_s, f_r, x_s, x_r, c_s, c_r,
     a_s, a_r, b_s, b_r, z_s, z_r, t_s, t_r,
@@ -33,7 +35,7 @@
     enc = k_ref.shape[2]
     enc_all = enc * RING * ROWS
     width = enc_ref.shape[1]
-    half = width // 2
+    quarter = width // 4
     piece = width // (RING * ROWS)
     yh_count = low_count // 2
 
@@ -97,7 +99,7 @@
                     own_s.at[layer, n],
                 )
             )
-    for copy in own_kv + own + own_w:
+    for copy in own_kv + own:
         copy.start()
 
     pl.semaphore_wait(barrier, len(others) + len(low_dps) + len(z_dps) + 1)
@@ -154,6 +156,9 @@
             if layer == 0 and slot == 1:
                 for copy in w_copies:
                     copy.start()
+
+    for copy in own_w:
+        copy.start()
 
     final = enc_ref[...].astype(jnp.float32)
     inv[...] = lax.rsqrt(jnp.mean(final * final, axis=-1, keepdims=True) + 1e-6)
@@ -244,85 +249,84 @@
             handed.start()
 
     own_depth = 2 * layers * LANES
-    tile = min(512, half)
-
-    def project(first, grads, depth_start, add):
+    tile = min(512, quarter)
+
+    def project(part_at, pieces, add):
         def one(index, carry):
-            at = first + index
-            weights = w[columns(at, tile), pl.ds(depth_start, own_depth)]
-            terms = lax.dot_general(
-                grads, weights, TRANSPOSED, preferred_element_type=jnp.float32
-            ).reshape(RING, enc, tile)
-            if add:
-                terms = terms + part[:, :, columns(at, tile)]
-            part[:, :, columns(at, tile)] = terms
+            at = columns(part_at * (quarter // tile) + index, tile)
+            terms = part[:, :, at].reshape(RING * enc, tile) if add else 0.0
+            for grads, start, depth in pieces:
+                terms = terms + lax.dot_general(
+                    grads, w[at, pl.ds(start, depth)], TRANSPOSED, preferred_element_type=jnp.float32
+                )
+            part[:, :, at] = terms.reshape(RING, enc, tile)
             return carry
 
-        lax.fori_loop(0, half // tile, one, 0)
-
-    mine = g_own[y]
-    project(0, mine, 0, False)
-    project(half // tile, mine, 0, False)
+        lax.fori_loop(0, quarter // tile, one, 0)
+
+    last_depth = 2 * LANES
+    early_depth = own_depth - last_depth
+    for exchange in exchanges[:-1]:
+        exchange.wait_recv()
     handed.wait()
-    for exchange in exchanges:
-        exchange.wait_recv()
-    theirs = g_far[...]
+    early = (
+        (g_own[y], 0, own_depth),
+        (g_far[:, pl.ds(0, early_depth)], own_depth, early_depth),
+    )
+    for at in PARTS:
+        project(at, early, False)
+    exchanges[-1].wait_recv()
+    late = ((g_far[:, pl.ds(early_depth, last_depth)], own_depth + early_depth, last_depth),)
 
     hops = {}
 
-    def term(dx, side_of):
-        return part[lax.rem(x + dx + RING, RING), :, pl.ds(side_of * half, half)]
-
-    def hop(chain, k):
-        way, side_of, length, first = CHAINS[chain]
-        total = term(way * (length - k), side_of)
+    def term(dx, at):
+        return part[lax.rem(x + dx + RING, RING), :, pl.ds(at * quarter, quarter)]
+
+    def hop(at, left, k):
+        way = -1 if left else 1
+        length = HOPS[at][left]
+        slot = FIRST[at][left] + k
+        total = term(way * (length - k), at)
         if k:
-            hops[chain, k - 1].wait_recv()
-            total = total + c_recv[first + k - 1].astype(jnp.float32)
-        c_send[first + k] = total.astype(jnp.bfloat16)
+            hops[at, left, k - 1].wait_recv()
+            total = total + c_recv[slot - 1].astype(jnp.float32)
+        c_send[slot] = total.astype(jnp.bfloat16)
         copy = pltpu.make_async_remote_copy(
-            c_send.at[first + k],
-            c_recv.at[first + k],
-            c_s.at[first + k],
-            c_r.at[first + k],
+            c_send.at[slot],
+            c_recv.at[slot],
+            c_s.at[slot],
+            c_r.at[slot],
             device_id={"seq": member(way, 0)},
             device_id_type=MESH,
         )
         copy.start()
-        hops[chain, k] = copy
-
-    project(0, theirs, own_depth, True)
-    hop(0, 0)
-    hop(3, 0)
-    project(half // tile, theirs, own_depth, True)
-    hop(1, 0)
-    hop(2, 0)
+        hops[at, left, k] = copy
+
+    for at in PARTS:
+        project(at, late, True)
+        hop(at, 0, 0)
+        hop(at, 1, 0)
     for copy in kv_copies + tok_copies + exchanges:
         copy.wait_send()
     for k in range(1, 4):
-        hop(0, k)
-        hop(1, k)
-        if k < 3:
-            hop(2, k)
-            hop(3, k)
-
-    arrived = []
-    for side_of in range(2):
-        total = term(0, side_of)
-        for chain, (way, chain_side, length, first) in enumerate(CHAINS):
-            if chain_side == side_of:
-                hops[chain, length - 1].wait_recv()
-                total = total + c_recv[first + length - 1].astype(jnp.float32)
-        arrived.append(total)
+        for at in PARTS:
+            for left in range(2):
+                if k < HOPS[at][left]:
+                    hop(at, left, k)
 
     a_copies = []
-    for side_of in range(2):
-        state = arrived[side_of]
-        cols = pl.ds(side_of * half, half)
-        part[0, :, cols] = state
+    for at in PARTS:
+        state = term(0, at)
+        for left in range(2):
+            last = HOPS[at][left] - 1
+            hops[at, left, last].wait_recv()
+            state = state + c_recv[FIRST[at][left] + last].astype(jnp.float32)
+        cols = pl.ds(at * quarter, quarter)
+        final_state[:, cols] = state
         gains = jnp.sum(state * normed[:, cols], axis=0, keepdims=True)
-        for s in range(RING):
-            a_send[side_of * RING + s] = gains[:, s * piece : (s + 1) * piece]
+        for s in range(quarter // piece):
+            a_send[at * (quarter // piece) + s] = gains[:, s * piece : (s + 1) * piece]
     for j, (dx, dy) in enumerate(others):
         to = member(dx, dy)
         copy = pltpu.make_async_remote_copy(
@@ -336,7 +340,7 @@
         copy.start()
         a_copies.append(copy)
 
-    state = part[0]
+    state = final_state[...]
     scaled = gain_ref[...] * state
     mean = jnp.mean(scaled * normed[...], axis=-1, keepdims=True)
     out_ref[...] = (inv[...] * (scaled - normed[...] * mean)).astype(jnp.bfloat16)
@@ -393,12 +397,23 @@
         gout_ref[:, pl.ds(s * piece, piece)] = t_recv[s]
 
 
+def hand_over(grads_in, gains_in, grads_out, gains_out, sems):
+    copies = (
+        pltpu.make_async_copy(grads_in, grads_out, sems.at[0]),
+        pltpu.make_async_copy(gains_in, gains_out, sems.at[1]),
+    )
+    for copy in copies:
+        copy.start()
+    for copy in copies:
+        copy.wait()
+
+
 def body(low_count, z_count, enc_final, norm_gain, q, g, k, v, kw, vw):
     enc, width = enc_final.shape[1:]
     layers, _, dec, _ = q.shape
     group = RING * ROWS
     enc_all = enc * group
-    half = width // 2
+    quarter = width // 4
     piece = width // group
     bf, f32 = jnp.bfloat16, jnp.float32
     dma = pltpu.SemaphoreType.DMA
@@ -425,9 +440,10 @@
             vmem((enc_all // ROWS, 2 * layers * LANES), bf),
             vmem((RING, enc, width), f32),
             vmem((enc, width), f32),
+            vmem((enc, width), f32),
             vmem((enc, 1), f32),
-            vmem((CHAIN_SLOTS, enc, half), bf),
-            vmem((CHAIN_SLOTS, enc, half), bf),
+            vmem((CHAIN_SLOTS, enc, quarter), bf),
+            vmem((CHAIN_SLOTS, enc, quarter), bf),
             vmem((group, 1, piece), f32),
             vmem((group, 1, piece), f32),
             vmem((1, piece), f32),
@@ -461,7 +477,14 @@
             collective_id=0, has_side_effects=True, vmem_limit_bytes=56 * 2**20
         ),
     )(enc_final[0], norm_gain[None], q, g, k, v, kw, vw)
-    return outs[0][None], outs[1][0]
+    grads, gains = pl.pallas_call(
+        hand_over,
+        out_shape=tuple(jax.ShapeDtypeStruct(o.shape, o.dtype) for o in outs),
+        in_specs=[pl.BlockSpec(memory_space=pl.ANY)] * 2,
+        out_specs=(pl.BlockSpec(memory_space=pl.ANY),) * 2,
+        scratch_shapes=[dma((2,))],
+    )(*outs)
+    return grads[None], gains[0]
 
 
 def solution(mesh):

time: 131 us -> 134 us (1.023)
  Pallas kernels: 127 us -> 133 us
  local copies, waits for them, and re-layouts: 2.94 us -> 0 us
    pallas_call x0 -> x1, Pallas kernels: none -> 7.57 us  [body(): pl.pallas_call(hand_over, out_shape=tuple((jax.ShapeDtypeStruct(o.shape,...]
    unnamed x2 -> x0, local copies, waits for them, and re-layouts: 2.94 us -> none
    pallas_call x1, Pallas kernels: 127 us -> 126 us  [body(): pl.pallas_call(functools.partial(kernel, low_count, z_count), out_shape=(...]
where the time goes in v2:
time: 134 us
  Pallas kernels  133 us (99%)
    pallas_call x1, Pallas kernels, body(): pl.pallas_call(functools.partial(kernel, low_count, z_count), out_shape=(...  126 us
    pallas_call x1, Pallas kernels, body(): pl.pallas_call(hand_over, out_shape=tuple((jax.ShapeDtypeStruct(o.shape,...  7.57 us

profile of v2, /device:TPU:1, one launch (start us, length us, event | category | flops | bytes accessed | tf_op | source)
XLA Modules:
  0.0 133.8 jit_solution(826683672063543349)
XLA Ops:
  0.6 125.6 %shard_map.95 = (bf16[24,4096]{1,0:T(8,128)(2,1)}, f32[1,4096]{1,0:T(1,128)}) custom-call(bf16[24,4096]{1,0:T(8,128)(2,1)} %bitcast.4, f32[1,4096]{1,0:T(1,128)} %bitcast.5, bf16[2,1,128,2048]{3,2,1,0:T(8,128)(2,1)} %q_ref.1, bf16[2,1,128,2048]{3,2,1,0:T(8,128)(2,1)} %g_ref.1, bf16[2,1,24,2048]{3,2,1,0:T(8,128)(2,1)} %k_ref.1, ...), custom_call_target="tpu_custom_call" | custom-call | tf_op jit(solution)/shard_map/pallas_call | solution.py:421
  126.2 7.6 %shard_map.96 = (bf16[24,4096]{1,0:T(8,128)(2,1)}, f32[1,4096]{1,0:T(1,128)}) custom-call(bf16[24,4096]{1,0:T(8,128)(2,1)} %get-tuple-element.6.grads_in, f32[1,4096]{1,0:T(1,128)} %get-tuple-element.7.gains_in), custom_call_target="tpu_custom_call" | custom-call | tf_op jit(solution)/shard_map/pallas_call | solution.py:480

commit v3 on v2

--- a/solution.py
+++ b/solution.py
@@ -13,9 +13,9 @@
 RING = 8
 ROWS = 2
 SHIFTS = (0, 4, 3, 5, 2, 6, 1, 7)
-PARTS = (0, 2, 1, 3)
-HOPS = ((4, 3), (4, 3), (3, 4), (3, 4))
-FIRST = tuple(tuple(sum(h[0] + h[1] for h in HOPS[:p]) + d * HOPS[p][0] for d in (0, 1)) for p in range(4))
+PARTS = (0, 4, 1, 5, 2, 6, 3, 7)
+HOPS = ((4, 3),) * 4 + ((3, 4),) * 4
+FIRST = tuple(tuple(sum(h[0] + h[1] for h in HOPS[:p]) + d * HOPS[p][0] for d in (0, 1)) for p in range(len(HOPS)))
 CHAIN_SLOTS = sum(h[0] + h[1] for h in HOPS)
 
 TRANSPOSED = (((1,), (1,)), ((), ()))
@@ -35,7 +35,7 @@
     enc = k_ref.shape[2]
     enc_all = enc * RING * ROWS
     width = enc_ref.shape[1]
-    quarter = width // 4
+    strip = width // len(PARTS)
     piece = width // (RING * ROWS)
     yh_count = low_count // 2
 
@@ -249,11 +249,11 @@
             handed.start()
 
     own_depth = 2 * layers * LANES
-    tile = min(512, quarter)
+    tile = min(512, strip)
 
     def project(part_at, pieces, add):
         def one(index, carry):
-            at = columns(part_at * (quarter // tile) + index, tile)
+            at = columns(part_at * (strip // tile) + index, tile)
             terms = part[:, :, at].reshape(RING * enc, tile) if add else 0.0
             for grads, start, depth in pieces:
                 terms = terms + lax.dot_general(
@@ -262,7 +262,7 @@
             part[:, :, at] = terms.reshape(RING, enc, tile)
             return carry
 
-        lax.fori_loop(0, quarter // tile, one, 0)
+        lax.fori_loop(0, strip // tile, one, 0)
 
     last_depth = 2 * LANES
     early_depth = own_depth - last_depth
@@ -281,7 +281,7 @@
     hops = {}
 
     def term(dx, at):
-        return part[lax.rem(x + dx + RING, RING), :, pl.ds(at * quarter, quarter)]
+        return part[lax.rem(x + dx + RING, RING), :, pl.ds(at * strip, strip)]
 
     def hop(at, left, k):
         way = -1 if left else 1
@@ -307,8 +307,6 @@
         project(at, late, True)
         hop(at, 0, 0)
         hop(at, 1, 0)
-    for copy in kv_copies + tok_copies + exchanges:
-        copy.wait_send()
     for k in range(1, 4):
         for at in PARTS:
             for left in range(2):
@@ -322,11 +320,11 @@
             last = HOPS[at][left] - 1
             hops[at, left, last].wait_recv()
             state = state + c_recv[FIRST[at][left] + last].astype(jnp.float32)
-        cols = pl.ds(at * quarter, quarter)
+        cols = pl.ds(at * strip, strip)
         final_state[:, cols] = state
         gains = jnp.sum(state * normed[:, cols], axis=0, keepdims=True)
-        for s in range(quarter // piece):
-            a_send[at * (quarter // piece) + s] = gains[:, s * piece : (s + 1) * piece]
+        for s in range(strip // piece):
+            a_send[at * (strip // piece) + s] = gains[:, s * piece : (s + 1) * piece]
     for j, (dx, dy) in enumerate(others):
         to = member(dx, dy)
         copy = pltpu.make_async_remote_copy(
@@ -344,6 +342,9 @@
     scaled = gain_ref[...] * state
     mean = jnp.mean(scaled * normed[...], axis=-1, keepdims=True)
     out_ref[...] = (inv[...] * (scaled - normed[...] * mean)).astype(jnp.bfloat16)
+
+    for copy in kv_copies + tok_copies + exchanges:
+        copy.wait_send()
 
     total = a_send[seq]
     for copy in a_copies:
@@ -376,7 +377,7 @@
     total, b_copies = everyone(total, b_send, b_recv, low, low_dps, b_s, b_r)
     total, z_copies = everyone(total, z_send, z_recv, z, z_dps, z_s, z_r)
 
-    t_recv[seq] = total * (1.0 / (low_count * z_count))
+    t_recv[seq] = total
     t_copies = []
     for j, (dx, dy) in enumerate(others):
         copy = pltpu.make_async_remote_copy(
@@ -397,23 +398,12 @@
         gout_ref[:, pl.ds(s * piece, piece)] = t_recv[s]
 
 
-def hand_over(grads_in, gains_in, grads_out, gains_out, sems):
-    copies = (
-        pltpu.make_async_copy(grads_in, grads_out, sems.at[0]),
-        pltpu.make_async_copy(gains_in, gains_out, sems.at[1]),
-    )
-    for copy in copies:
-        copy.start()
-    for copy in copies:
-        copy.wait()
-
-
 def body(low_count, z_count, enc_final, norm_gain, q, g, k, v, kw, vw):
     enc, width = enc_final.shape[1:]
     layers, _, dec, _ = q.shape
     group = RING * ROWS
     enc_all = enc * group
-    quarter = width // 4
+    strip = width // len(PARTS)
     piece = width // group
     bf, f32 = jnp.bfloat16, jnp.float32
     dma = pltpu.SemaphoreType.DMA
@@ -442,8 +432,8 @@
             vmem((enc, width), f32),
             vmem((enc, width), f32),
             vmem((enc, 1), f32),
-            vmem((CHAIN_SLOTS, enc, quarter), bf),
-            vmem((CHAIN_SLOTS, enc, quarter), bf),
+            vmem((CHAIN_SLOTS, enc, strip), bf),
+            vmem((CHAIN_SLOTS, enc, strip), bf),
             vmem((group, 1, piece), f32),
             vmem((group, 1, piece), f32),
             vmem((1, piece), f32),
@@ -477,14 +467,8 @@
             collective_id=0, has_side_effects=True, vmem_limit_bytes=56 * 2**20
         ),
     )(enc_final[0], norm_gain[None], q, g, k, v, kw, vw)
-    grads, gains = pl.pallas_call(
-        hand_over,
-        out_shape=tuple(jax.ShapeDtypeStruct(o.shape, o.dtype) for o in outs),
-        in_specs=[pl.BlockSpec(memory_space=pl.ANY)] * 2,
-        out_specs=(pl.BlockSpec(memory_space=pl.ANY),) * 2,
-        scratch_shapes=[dma((2,))],
-    )(*outs)
-    return grads[None], gains[0]
+    grads, gains = outs
+    return grads[None], gains[0] * (1.0 / (low_count * z_count))
 
 
 def solution(mesh):

time: 134 us -> 129 us (0.963)
  Pallas kernels: 133 us -> 126 us
  local copies, waits for them, and re-layouts: 0 us -> 1.62 us
  other arithmetic: 0 us -> 1.34 us
    pallas_call x1 -> x0, Pallas kernels: 7.57 us -> none  [body(): pl.pallas_call(hand_over, out_shape=tuple((jax.ShapeDtypeStruct(o.shape,...]
    unnamed x0 -> x1, local copies, waits for them, and re-layouts: none -> 1.62 us
where the time goes in v3:
time: 129 us
  Pallas kernels  126 us (98%)
  local copies, waits for them, and re-layouts  1.62 us (1%)
  other arithmetic  1.34 us (1%)
    pallas_call x1, Pallas kernels, body(): pl.pallas_call(functools.partial(kernel, low_count, z_count), out_shape=(...  126 us

profile of v3, /device:TPU:1, one launch (start us, length us, event | category | flops | bytes accessed | tf_op | source)
XLA Modules:
  0.0 129.1 jit_solution(12009913715505466688)
XLA Ops:
  0.6 125.5 %shard_map.95 = (bf16[24,4096]{1,0:T(8,128)(2,1)}, f32[1,4096]{1,0:T(1,128)}) custom-call(bf16[24,4096]{1,0:T(8,128)(2,1)} %bitcast.5, f32[1,4096]{1,0:T(1,128)} %bitcast.6, bf16[2,1,128,2048]{3,2,1,0:T(8,128)(2,1)} %q_ref.1, bf16[2,1,128,2048]{3,2,1,0:T(8,128)(2,1)} %g_ref.1, bf16[2,1,24,2048]{3,2,1,0:T(8,128)(2,1)} %k_ref.1, ...), custom_call_target="tpu_custom_call" | custom-call | tf_op jit(solution)/shard_map/pallas_call | solution.py:411
  126.2 1.3 %broadcast_multiply_fusion = f32[1,4096]{1,0:T(1,128)} fusion(f32[1,4096]{1,0:T(1,128)} %get-tuple-element.5), kind=kLoop, calls=%fused_computation | loop fusion | flops 4096 | bytes 32768 | tf_op jit(solution)/shard_map/mul | solution.py:471
  127.5 1.6 %copy.11 = bf16[1,24,4096]{2,1,0:T(8,128)(2,1)} copy(bf16[1,24,4096]{2,1,0:T(8,128)(2,1)} %bitcast.4) | data formatting | bytes 393216
